TPU v7x, 32 devices: a whole 2x2x4 slice. The times are simulated.
32 devices in a mesh: grp: 2 (over x), row: 16 (over z, y, core).
Axes of the slice: x: 2, y: 2, z: 4, core: 2. Of those that a mesh axis runs over, the one named last changes fastest.
Arguments:
- slot_pairs: int32 [16512, 2], P(('grp', 'row')), parts along dimension 0, may hold values from -1 to 127, as said below
- lag_table: int32 [256, 128], P('grp'), parts along dimension 0, may hold values from 0 to 3, as said below
- kernel: float32 [16512, 128, 128], P(('grp', 'row')), parts along dimension 0, may hold values from -0.046875 to 0.046875
- history: float32 [8, 32, 16384], P('grp', None, 'row'), parts along dimension 0, may hold values from -6 to 6
Outputs:
- field: float32 [64, 16384], P('grp', 'row'), parts along dimension 0
There are 2 independent parts, one for each index of `grp`. A program takes and returns all parts, laid end to end along the dimension named above; each array names one. Nothing has to cross between parts.
Inputs may be any that keep to these rules, and one draw needn't show every extreme that they name: `slot_pairs`: each pair (i, j) with i <= j < 128 stands in exactly one slot, in an order drawn from the seed; every other slot holds -1 in both columns. `lag_table`: symmetric.
All inputs are finite; a program needn't handle non-finite values.
Results may differ from a plain program's by a relative error of at most 0.0003.
Values sent between devices are 32-bit elements; how exact they have to be, the bound alone decides.
A program may use at most 128 MiB of HBM per device.

v0:
```python
import jax
import jax.numpy as jnp
from jax import lax
from jax.sharding import PartitionSpec as P

N = 16384
EXC = 32
LAGS = 4
BLOCK = 128


def body(slot_pairs, lag_table, kernel, history):
    n_blocks = N // BLOCK
    row_ids = jnp.maximum(slot_pairs[:, 0], 0)
    col_ids = jnp.maximum(slot_pairs[:, 1], 0)
    live_mask = (slot_pairs[:, 0] >= 0).astype(jnp.float32)
    off_diag = live_mask * (row_ids != col_ids).astype(jnp.float32)
    lag_ids = lag_table[row_ids, col_ids]
    totals = jnp.zeros((EXC, n_blocks, BLOCK), jnp.float32)
    gathered = lax.all_gather(history, "row", axis=2, tiled=True)
    panels = gathered.reshape(LAGS, EXC, n_blocks, BLOCK)
    far_panels = jnp.transpose(panels[lag_ids, :, col_ids, :], (1, 0, 2))
    near_panels = jnp.transpose(panels[lag_ids, :, row_ids, :], (1, 0, 2))
    direct = (
        jnp.einsum(
            "esb,sab->esa",
            far_panels,
            kernel,
            precision=lax.Precision.HIGHEST,
            preferred_element_type=jnp.float32,
        )
        * live_mask[None, :, None]
    )
    mirror = (
        jnp.einsum(
            "esb,sba->esa",
            near_panels,
            kernel,
            precision=lax.Precision.HIGHEST,
            preferred_element_type=jnp.float32,
        )
        * off_diag[None, :, None]
    )
    totals = totals.at[:, row_ids, :].add(direct)
    totals = totals.at[:, col_ids, :].add(mirror)
    partial_value = totals.reshape(EXC, N)
    field = lax.psum_scatter(partial_value, "row", scatter_dimension=1, tiled=True)
    return field


def solution(mesh):
    return jax.shard_map(
        body,
        mesh=mesh,
        in_specs=(
            P(("grp", "row"), None),
            P("grp", None),
            P(("grp", "row"), None, None),
            P("grp", None, "row"),
        ),
        out_specs=P("grp", "row"),
        check_vma=False,
    )
```

profile of v0, /device:TPU:0, one launch (start us, length us, event | category | flops | bytes accessed | tf_op | source)
XLA Modules:
  0.0 373.8 jit_solution(11706149027521548745)
XLA Ops:
  6.5 0.0 copy-start
  6.5 0.0 all-gather.2.cloned.1.call-start
  6.5 0.7 all-gather.2.cloned.1.call-update
  7.3 0.0 reduce-scatter.2.cloned.1.call-start
  7.3 0.8 or_reduce_fusion.2
  8.1 0.0 copy-done
  8.1 5.8 %gather_fusion = s32[516]{0:T(1024)S(1)} fusion(s32[128,128]{1,0:T(8,128)S(1)} %copy-done, s32[516]{0:T(1024)S(1)} %or_reduce_fusion.2), kind=kCustom, calls=%fused_computation | custom fusion | bytes 8256 | tf_op jit(solution)/shard_map/gather | solution.py:18
  13.9 0.7 fusion.8
  14.7 0.8 compare_reduce_fusion
  15.4 0.8 or_reduce_fusion
  16.3 70.9 %all-gather.2.cloned.1.call-done = f32[4,32,16384]{2,1,0:T(8,128)} async-done(((f32[4,32,1024]{2,1,0:T(8,128)}), f32[4,32,16384]{2,1,0:T(8,128)}) %all-gather.2.cloned.1.call-update) | async-done | bytes 8388624 | tf_op jit(solution)/shard_map/all_gather | solution.py:20
  87.2 7.8 %copy_bitcast_fusion = f32[4,32,128,128]{3,1,2,0:T(8,128)} fusion(f32[4,32,16384]{2,1,0:T(8,128)} %all-gather.2.cloned.1.call-done), kind=kLoop, calls=%fused_computation.9 | loop fusion | bytes 16777216 | tf_op jit(solution)/shard_map/reshape | solution.py:21
  95.0 13.0 %gather_fusion.1 = f32[516,32,128]{2,1,0:T(8,128)} fusion(f32[4,32,128,128]{3,1,2,0:T(8,128)} %copy_bitcast_fusion, s32[516]{0:T(1024)S(1)} %get-tuple-element.6), kind=kCustom, calls=%fused_computation.1 | custom fusion | bytes 16912416 | tf_op jit(solution)/shard_map/gather | solution.py:22
  108.0 13.0 %gather_fusion.2 = f32[516,32,128]{2,1,0:T(8,128)} fusion(f32[4,32,128,128]{3,1,2,0:T(8,128)} %copy_bitcast_fusion, s32[516]{0:T(1024)S(1)} %get-tuple-element.5), kind=kCustom, calls=%fused_computation.2 | custom fusion | bytes 16912416 | tf_op jit(solution)/shard_map/gather | solution.py:23
  121.0 0.0 copy-start.2
  121.0 57.2 %broadcast_multiply_fusion.1 = f32[516,32,128]{2,1,0:T(8,128)} fusion(f32[516]{0:T(1024)S(1)} %fusion.8, f32[516,128,128]{2,1,0:T(8,128)} %param.6, f32[516,32,128]{2,1,0:T(8,128)} %gather_fusion.1), kind=kOutput, calls=%fused_computation.11 | convolution fusion | flops 3248504832 | bytes 50726928 | tf_op jit(solution)/shard_map/esb,sab->esa/dot_general | solution.py:25
  178.3 0.0 copy-done.2
  178.3 33.2 %broadcast_multiply_fusion = f32[516,32,128]{2,1,0:T(8,128)} fusion(f32[516]{0:T(1024)S(1)} %broadcast_select_fusion, f32[516,128,128]{2,1,0:T(8,128)} %param.6, f32[516,32,128]{2,1,0:T(8,128)S(1)} %copy-done.2), kind=kOutput, calls=%fused_computation.10 | convolution fusion | flops 3248504832 | bytes 50726928 | tf_op jit(solution)/shard_map/esb,sba->esa/dot_general | solution.py:35
  211.5 0.2 broadcast_in_dim.2
  211.7 46.9 %scatter_fusion = f32[32,128,128]{2,0,1:T(8,128)S(1)} fusion(f32[32,128,128]{2,0,1:T(8,128)S(1)} %broadcast_in_dim.2, s32[516]{0:T(1024)S(1)} %get-tuple-element.7, f32[516,32,128]{2,1,0:T(8,128)} %broadcast_multiply_fusion.1), kind=kCustom, calls=%fused_computation.3 | custom fusion | flops 2113536 | bytes 25364496 | tf_op jit(solution)/shard_map/scatter-add | solution.py:44
  258.6 0.0 copy-start.1
  258.6 46.9 %scatter_fusion.1 = f32[32,128,128]{2,0,1:T(8,128)S(1)} fusion(f32[32,128,128]{2,0,1:T(8,128)S(1)} %scatter_fusion, s32[516]{0:T(1024)S(1)} %get-tuple-element.8, f32[516,32,128]{2,1,0:T(8,128)} %broadcast_multiply_fusion), kind=kCustom, calls=%fused_computation.4 | custom fusion | flops 2113536 | bytes 25364496 | tf_op jit(solution)/shard_map/scatter-add | solution.py:45
  305.5 1.5 copy_bitcast_fusion.1
  307.0 0.0 reduce-scatter.2.cloned.1.call-update
  307.0 60.0 %reduce-scatter.2.cloned.1.call-done = f32[32,1024]{1,0:T(8,128)} async-done(((f32[32,16384]{1,0:T(8,128)}), f32[32,1024]{1,0:T(8,128)}) %reduce-scatter.2.cloned.1.call-update) | async-done | bytes 131088 | tf_op jit(solution)/shard_map/reduce_scatter | solution.py:47
  367.0 0.0 copy-done.1
  (1 shorter events, 0.0 us)
Async XLA Ops:
  6.5 1.6 copy-start
  6.5 80.7 %all-gather.2.cloned.1.call-start = ((), (), s32[]{:S(2)}) async-start(), calls=%async_computation.1 | async-start | bytes 8912896 | tf_op jit(solution)/shard_map/all_gather | solution.py:20
  7.3 359.7 %reduce-scatter.2.cloned.1.call-start = ((), (), s32[]{:S(2)}) async-start(), calls=%async_computation.2 | async-start | bytes 2228224 | tf_op jit(solution)/shard_map/reduce_scatter | solution.py:47
  121.0 57.2 %copy-start.2 = (f32[516,32,128]{2,1,0:T(8,128)S(1)}, f32[516,32,128]{2,1,0:T(8,128)}, u32[]{:S(2)}) copy-start(f32[516,32,128]{2,1,0:T(8,128)} %gather_fusion.2) | copy-start | bytes 25362436
  258.6 108.4 %copy-start.1 = (s32[128,128]{1,0:T(8,128)S(1)}, s32[128,128]{1,0:T(8,128)}, u32[]{:S(2)}) copy-start(s32[128,128]{1,0:T(8,128)} %param.5) | copy-start | bytes 196612
Sparse Core Ops, SparseCore 0:
  9.6 77.6 all-gather.1
  307.1 59.8 reduce-scatter.1
where the time goes:
time: 376 us; the launch traced here: 374 us
  waiting for transfers between devices  132 us (35%)
  other arithmetic  96.8 us (26%)
  matrix products  90.4 us (24%)
  local copies, waits for them, and re-layouts  41.4 us (11%)
  between operations  13.5 us (4%)
    all_gather x1, waiting for transfers between devices, body(): gathered = lax.all_gather(history, 'row', axis=2, tiled=True)  70.9 us
    reduce_scatter x1, waiting for transfers between devices, body(): lax.psum_scatter(partial_value, 'row', scatter_dimension=1, tiled=True)  60 us
    dot_general x1, matrix products, body(): jnp.einsum('esb,sab->esa', far_panels, kernel, precision=lax.Precision.HI...  57.2 us
    scatter-add x1, other arithmetic, body(): totals = totals.at[:, col_ids, :].add(mirror)  46.9 us
    scatter-add x1, other arithmetic, body(): totals = totals.at[:, row_ids, :].add(direct)  46.9 us
    dot_general x1, matrix products, body(): jnp.einsum('esb,sba->esa', near_panels, kernel, precision=lax.Precision.H...  33.2 us
    gather x1, local copies, waits for them, and re-layouts, body(): far_panels = jnp.transpose(panels[lag_ids, :, col_ids, :], (1, 0, 2))  13 us
    gather x1, local copies, waits for them, and re-layouts, body(): near_panels = jnp.transpose(panels[lag_ids, :, row_ids, :], (1, 0, 2))  13 us
  transfers between devices with their start and end apart: 2, of which 2 were waited for; matrix products, arithmetic and copies ran while one was open for 2% of the time, Pallas kernels for 0%

commit v1 on v0

v1 whole, which is shorter than its diff:
```python
import functools

import jax
import jax.numpy as jnp
from jax import lax
from jax.experimental import pallas as pl
from jax.experimental.pallas import tpu as pltpu
from jax.sharding import PartitionSpec as P

MESH = pl.DeviceIdType.MESH
MIB = 1024 * 1024


def grid_of(rows):
    chips = rows // 2
    side_b = 1
    while side_b * side_b * 4 <= chips:
        side_b *= 2
    return chips // side_b, side_b


def place(side_b):
    r = lax.axis_index("row")
    core = lax.rem(r, 2)
    chip = r // 2
    return r, chip // side_b, lax.rem(chip, side_b), core


def greet(side_a, side_b, a, b, core):
    barrier = pltpu.get_barrier_semaphore()

    def signal(row):
        pl.semaphore_signal(barrier, inc=1, device_id={"row": row}, device_id_type=MESH)

    for d in range(1, side_a):
        signal((lax.rem(a + d, side_a) * side_b + b) * 2 + core)
    for d in range(1, side_b):
        signal((a * side_b + lax.rem(b + d, side_b)) * 2 + core)
    signal((a * side_b + b) * 2 + 1 - core)
    pl.semaphore_wait(barrier, side_a + side_b - 1)


def gather_kernel(side_a, side_b, group, h_ref, g_ref, own, local_sem, z_sem, y_sem, c_sem, recv_sem):
    r, a, b, core = place(side_b)
    lags = h_ref.shape[0]
    width = g_ref.shape[3]
    per = h_ref.shape[2] // width
    parts = lags // group
    greet(side_a, side_b, a, b, core)
    for k in range(lags):
        for m in range(per):
            own[k, m] = h_ref[k, :, m * width : (m + 1) * width]

    def row_of(a_, b_, c_):
        return (a_ * side_b + b_) * 2 + c_

    def chunk(k, row):
        return g_ref.at[pl.ds(k * group, group), pl.ds(row * per, per)]

    def copy(k, origin, target, send, mine=False):
        src = own.at[pl.ds(k * group, group)] if mine else chunk(k, origin)
        return pltpu.make_async_remote_copy(
            src_ref=src,
            dst_ref=chunk(k, origin),
            send_sem=send,
            recv_sem=recv_sem.at[k, origin],
            device_id={"row": target},
            device_id_type=MESH,
        )

    sent = []

    def send(*args, **kw):
        c = copy(*args, **kw)
        c.start()
        sent.append(c)

    def arrived(k, origin):
        copy(k, origin, row_of(a, b, 1 - core), c_sem.at[k, 0]).wait_recv()

    local = []
    for k in range(parts):
        for d in range(1, side_a):
            send(k, r, row_of(lax.rem(a + d, side_a), b, core), z_sem.at[k, d], mine=True)
        for e in range(1, side_b):
            send(k, r, row_of(a, lax.rem(b + e, side_b), core), y_sem.at[k, 0, e], mine=True)
        send(k, r, row_of(a, b, 1 - core), c_sem.at[k, 0], mine=True)
        c = pltpu.make_async_copy(own.at[pl.ds(k * group, group)], chunk(k, r), local_sem.at[k])
        c.start()
        local.append(c)

    def column(k):
        for d in range(1, side_a):
            origin = row_of(lax.rem(a + d, side_a), b, core)
            arrived(k, origin)
            for e in range(1, side_b):
                send(k, origin, row_of(a, lax.rem(b + e, side_b), core), y_sem.at[k, d, e])
            send(k, origin, row_of(a, b, 1 - core), c_sem.at[k, d])

    def across(k):
        for d in range(side_a):
            for e in range(1, side_b):
                origin = row_of(lax.rem(a + d, side_a), lax.rem(b + e, side_b), core)
                arrived(k, origin)
                send(k, origin, row_of(a, b, 1 - core), c_sem.at[k, e * side_a + d])

    for k in range(parts):
        column(k)
        if k > 0:
            across(k - 1)
    across(parts - 1)
    for k in range(parts):
        for d in range(side_a):
            for e in range(side_b):
                arrived(k, row_of(lax.rem(a + d, side_a), lax.rem(b + e, side_b), 1 - core))
    for c in local:
        c.wait()
    for c in sent:
        c.wait_send()


def gather_history(history, rows, width):
    lags, exc, local = history.shape
    per = local // width
    side_a, side_b = grid_of(rows)
    group = 1 if rows <= 16 else lags
    parts = lags // group
    return pl.pallas_call(
        functools.partial(gather_kernel, side_a, side_b, group),
        out_shape=jax.ShapeDtypeStruct((lags, rows * per, exc, width), jnp.float32),
        in_specs=[pl.BlockSpec(memory_space=pltpu.VMEM)],
        out_specs=pl.BlockSpec(memory_space=pl.ANY),
        scratch_shapes=[
            pltpu.VMEM((lags, per, exc, width), jnp.float32),
            pltpu.SemaphoreType.DMA((parts,)),
            pltpu.SemaphoreType.DMA((parts, side_a)),
            pltpu.SemaphoreType.DMA((parts, side_a, side_b)),
            pltpu.SemaphoreType.DMA((parts, side_a * side_b)),
            pltpu.SemaphoreType.DMA((parts, rows)),
        ],
        compiler_params=pltpu.CompilerParams(collective_id=0, has_side_effects=True),
        name="gather_history",
    )(history)


def split(x):
    hi = x.astype(jnp.bfloat16)
    lo = (x - hi.astype(jnp.float32)).astype(jnp.bfloat16)
    return hi, lo


def product_kernel(slots, pairs, lag, g_ref, k_ref, t_ref):
    step = pl.program_id(0)
    exc = g_ref.shape[2]
    blocks = g_ref.shape[1]

    @pl.when(step == 0)
    def _():
        t_ref[...] = jnp.zeros_like(t_ref)

    def panel(k, col):
        hi, lo = split(g_ref[k, col])
        return jnp.concatenate(
            [jnp.concatenate([hi, hi], axis=1), jnp.concatenate([lo, lo], axis=1)], axis=0
        )

    for q in range(slots):
        s = step * slots + q
        i = pairs[2 * s]
        j = pairs[2 * s + 1]
        live = i >= 0
        row = jnp.maximum(i, 0)
        col = jnp.maximum(j, 0)
        k = lag[row, col]
        hi, lo = split(k_ref[q])
        far = lax.dot_general(
            panel(k, col),
            jnp.concatenate([hi, lo], axis=1),
            (((1,), (1,)), ((), ())),
            preferred_element_type=jnp.float32,
        )
        near = lax.dot_general(
            panel(k, row),
            jnp.concatenate([hi, lo], axis=0),
            (((1,), (0,)), ((), ())),
            preferred_element_type=jnp.float32,
        )
        to_row = jnp.where(live, i, blocks)
        to_col = jnp.where(jnp.logical_and(live, i != j), j, blocks)
        t_ref[to_row] += far[:exc] + far[exc:]
        t_ref[to_col] += near[:exc] + near[exc:]


def products(slot_pairs, lag_table, kernel, panels):
    n = kernel.shape[0]
    width = kernel.shape[1]
    lags, blocks, exc, _ = panels.shape
    slots = max(d for d in range(1, 13) if n % d == 0)
    return pl.pallas_call(
        functools.partial(product_kernel, slots),
        out_shape=jax.ShapeDtypeStruct((blocks + 1, exc, width), jnp.float32),
        grid_spec=pltpu.PrefetchScalarGridSpec(
            num_scalar_prefetch=2,
            grid=(n // slots,),
            in_specs=[
                pl.BlockSpec(panels.shape, lambda s, *_: (0, 0, 0, 0), pipeline_mode=pl.Buffered(1)),
                pl.BlockSpec((slots, width, width), lambda s, *_: (s, 0, 0)),
            ],
            out_specs=pl.BlockSpec((blocks + 1, exc, width), lambda s, *_: (0, 0, 0)),
        ),
        compiler_params=pltpu.CompilerParams(
            dimension_semantics=("arbitrary",), vmem_limit_bytes=40 * MIB
        ),
        cost_estimate=pl.CostEstimate(
            flops=n * width * width * exc * 16,
            bytes_accessed=n * width * width * 4 + panels.size * 4,
            transcendentals=0,
        ),
        name="block_products",
    )(slot_pairs.reshape(-1), lag_table, panels, kernel)


def scatter_kernel(side_a, side_b, per, t_ref, o_ref, buf1, buf2, buf3, sum2, sum3, s1, r1, s2, r2, s3, r3):
    r, a, b, core = place(side_b)
    width = t_ref.shape[2]
    greet(side_a, side_b, a, b, core)

    def row_of(a_, b_, c_):
        return (a_ * side_b + b_) * 2 + c_

    def part(row):
        return pl.ds(row * per, per)

    def remote(src, dst, ssem, rsem, target):
        return pltpu.make_async_remote_copy(
            src_ref=src, dst_ref=dst, send_sem=ssem, recv_sem=rsem,
            device_id={"row": target}, device_id_type=MESH,
        )

    sent = []
    order = [(d, e) for e in range(side_b - 1, -1, -1) for d in list(range(1, side_a)) + [0]]

    def at(d, e):
        return lax.rem(a + d, side_a), lax.rem(b + e, side_b)

    peer = row_of(a, b, 1 - core)

    def to_core(d, e):
        a_, b_ = at(d, e)
        chip = a_ * side_b + b_
        return remote(
            t_ref.at[part(row_of(a_, b_, 1 - core))], buf1.at[chip], s1.at[chip], r1.at[chip], peer
        )

    for d, e in order:
        c = to_core(d, e)
        c.start()
        sent.append(c)

    def core_sum(d, e):
        a_, b_ = at(d, e)
        to_core(d, e).wait_recv()
        return t_ref[part(row_of(a_, b_, core))] + buf1[a_ * side_b + b_]

    for d, e in order:
        a_, b_ = at(d, e)
        if e > 0:
            sum2[e - 1, d] = core_sum(d, e)
            c = remote(sum2.at[e - 1, d], buf2.at[b, a_], s2.at[e - 1, d], r2.at[b, a_], row_of(a, b_, core))
            c.start()
            sent.append(c)
            continue
        total = core_sum(d, 0)
        for e2 in range(1, side_b):
            from_b = lax.rem(b + e2, side_b)
            remote(
                sum2.at[e2 - 1, d], buf2.at[from_b, a_], s2.at[e2 - 1, d], r2.at[from_b, a_], row_of(a, from_b, core)
            ).wait_recv()
            total = total + buf2[from_b, a_]
        if d > 0:
            sum3[d] = total
            c = remote(sum3.at[d], buf3.at[a], s3.at[d], r3.at[a], row_of(a_, b, core))
            c.start()
            sent.append(c)
            continue
        sum3[0] = total
    for d in range(1, side_a):
        from_a = lax.rem(a + d, side_a)
        remote(sum3.at[d], buf3.at[from_a], s3.at[d], r3.at[from_a], row_of(from_a, b, core)).wait_recv()
    for m in range(per):
        total = sum3[0, m]
        for d in range(1, side_a):
            total = total + buf3[lax.rem(a + d, side_a), m]
        o_ref[:, m * width : (m + 1) * width] = total
    for c in sent:
        c.wait_send()


def scatter_sum(totals, rows, blocks):
    _, exc, width = totals.shape
    per = blocks // rows
    side_a, side_b = grid_of(rows)
    chips = side_a * side_b
    dma = pltpu.SemaphoreType.DMA
    return pl.pallas_call(
        functools.partial(scatter_kernel, side_a, side_b, per),
        out_shape=jax.ShapeDtypeStruct((exc, per * width), jnp.float32),
        in_specs=[pl.BlockSpec(memory_space=pltpu.VMEM)],
        out_specs=pl.BlockSpec(memory_space=pltpu.VMEM),
        scratch_shapes=[
            pltpu.VMEM((chips, per, exc, width), jnp.float32),
            pltpu.VMEM((side_b, side_a, per, exc, width), jnp.float32),
            pltpu.VMEM((side_a, per, exc, width), jnp.float32),
            pltpu.VMEM((max(side_b - 1, 1), side_a, per, exc, width), jnp.float32),
            pltpu.VMEM((side_a, per, exc, width), jnp.float32),
            dma((chips,)),
            dma((chips,)),
            dma((max(side_b - 1, 1), side_a)),
            dma((side_b, side_a)),
            dma((side_a,)),
            dma((side_a,)),
        ],
        compiler_params=pltpu.CompilerParams(
            collective_id=1, has_side_effects=True, vmem_limit_bytes=24 * MIB
        ),
        name="scatter_sum",
    )(totals)


def body(rows, slot_pairs, lag_table, kernel, history):
    width = kernel.shape[1]
    panels = gather_history(history, rows, width)
    totals = products(slot_pairs, lag_table, kernel, panels)
    return scatter_sum(totals, rows, panels.shape[1])


def solution(mesh):
    return jax.shard_map(
        functools.partial(body, mesh.shape["row"]),
        mesh=mesh,
        in_specs=(
            P(("grp", "row"), None),
            P("grp", None),
            P(("grp", "row"), None, None),
            P("grp", None, "row"),
        ),
        out_specs=P("grp", "row"),
        check_vma=False,
    )
```

time: 376 us -> 135 us (0.36)
  waiting for transfers between devices: 132 us -> 0 us
  Pallas kernels: 0 us -> 129 us
  other arithmetic: 96.8 us -> 0 us
  matrix products: 90.4 us -> 0 us
  local copies, waits for them, and re-layouts: 41.4 us -> 5.06 us
  between operations: 13.5 us -> 0.06 us
    pallas_call x0 -> x3, Pallas kernels: none -> 129 us  [the longest x1 62.8 us: gather_history(): pl.pallas_call(functools.partial(gather_kernel, side_a, side_b, group), o...]
    scatter-add x2 -> x0, other arithmetic: 93.7 us -> none  [the longest x1 46.9 us: body(): totals = totals.at[:, col_ids, :].add(mirror)]
    dot_general x2 -> x0, matrix products: 90.4 us -> none  [the longest x1 57.2 us: body(): jnp.einsum('esb,sab->esa', far_panels, kernel, precision=lax.Precision.HI...]
    all_gather x1 -> x0, waiting for transfers between devices: 70.9 us -> none  [body(): gathered = lax.all_gather(history, 'row', axis=2, tiled=True)]
    reduce_scatter x1 -> x0, waiting for transfers between devices: 60 us -> none  [body(): lax.psum_scatter(partial_value, 'row', scatter_dimension=1, tiled=True)]
    gather x3 -> x0, local copies, waits for them, and re-layouts: 31.9 us -> none  [the longest x1 13 us: body(): far_panels = jnp.transpose(panels[lag_ids, :, col_ids, :], (1, 0, 2))]
    reshape x2 -> x1, local copies, waits for them, and re-layouts: 9.29 us -> 0.17 us  [products(): slot_pairs.reshape(-1)]
    unnamed x6, local copies, waits for them, and re-layouts: 0.01 us -> 4.9 us
  transfers between devices with their start and end apart: 2 -> 0, of which waited for: 2 -> 0; matrix products, arithmetic and copies ran while one was open for 2% -> 0% of each run, Pallas kernels for 0% -> 0%
where the time goes in v1:
time: 135 us; the launch traced here: 134 us
  Pallas kernels  129 us (96%)
  local copies, waits for them, and re-layouts  5.06 us (4%)
    pallas_call x1, Pallas kernels, gather_history(): pl.pallas_call(functools.partial(gather_kernel, side_a, side_b, group), o...  62.8 us
    pallas_call x1, Pallas kernels, products(): pl.pallas_call(functools.partial(product_kernel, slots), out_shape=jax.Sh...  38.4 us
    pallas_call x1, Pallas kernels, scatter_sum(): pl.pallas_call(functools.partial(scatter_kernel, side_a, side_b, per), ou...  28.1 us
    unnamed x6, local copies, waits for them, and re-layouts  4.9 us

profile of v1, /device:TPU:0, one launch (start us, length us, event | category | flops | bytes accessed | tf_op | source)
XLA Modules:
  0.0 134.4 jit_solution(972894675889675466)
XLA Ops:
  0.0 0.0 copy-start.1
  0.0 0.9 copy.5
  0.9 0.2 reshape.3.pairs
  1.0 62.8 %gather_history.1.g_ref = f32[4,128,32,128]{3,2,1,0:T(8,128)} custom-call(f32[4,32,1024]{2,1,0:T(8,128)} %h_ref.1), custom_call_target="tpu_custom_call" | custom-call | tf_op jit(solution)/shard_map/gather_history/pallas_call | solution.py:128
  63.9 0.0 copy-done.1
  63.9 0.0 copy-start
  63.9 3.4 %copy-done = f32[4,128,32,128]{3,2,1,0:T(8,128)S(1)} copy-done((f32[4,128,32,128]{3,2,1,0:T(8,128)S(1)}, f32[4,128,32,128]{3,2,1,0:T(8,128)}, u32[]{:S(2)}) %copy-start) | copy-done | bytes 8388632
  67.3 38.4 %block_products.1.t_ref = f32[129,32,128]{2,1,0:T(8,128)S(1)} custom-call(s32[1032]{0:T(1024)S(1)} %reshape.3.pairs, s32[128,128]{1,0:T(8,128)S(1)} %copy-done.1, f32[4,128,32,128]{3,2,1,0:T(8,128)S(1)} %copy-done, f32[516,128,128]{2,1,0:T(8,128)} %k_ref.1), custom_call_target="tpu_custom_call" | custom-call | flops 4328521728 | bytes 42205184 | tf_op jit(solution)/shard_map/block_products/pallas_call | solution.py:199
  105.6 28.1 %scatter_sum.1 = f32[32,1024]{1,0:T(8,128)S(1)} custom-call(f32[129,32,128]{2,1,0:T(8,128)S(1)} %block_products.1.t_ref), custom_call_target="tpu_custom_call" | custom-call | tf_op jit(solution)/shard_map/scatter_sum/pallas_call | solution.py:305
  133.8 0.7 copy.7
Async XLA Ops:
  0.0 63.9 %copy-start.1 = (s32[128,128]{1,0:T(8,128)S(1)}, s32[128,128]{1,0:T(8,128)}, u32[]{:S(2)}) copy-start(s32[128,128]{1,0:T(8,128)} %lag.1) | copy-start | bytes 196612
  63.9 3.4 %copy-start = (f32[4,128,32,128]{3,2,1,0:T(8,128)S(1)}, f32[4,128,32,128]{3,2,1,0:T(8,128)}, u32[]{:S(2)}) copy-start(f32[4,128,32,128]{3,2,1,0:T(8,128)} %gather_history.1.g_ref) | copy-start | bytes 25165828

commit v2 on v1

--- a/solution.py
+++ b/solution.py
@@ -68,41 +68,63 @@
             device_id_type=MESH,
         )
 
-    sent = []
-
-    def send(*args, **kw):
-        c = copy(*args, **kw)
-        c.start()
-        sent.append(c)
-
     def arrived(k, origin):
         copy(k, origin, row_of(a, b, 1 - core), c_sem.at[k, 0]).wait_recv()
 
+    def inside(a_):
+        return jnp.logical_and(a_ >= 0, a_ < side_a)
+
+    hops = [(1, 0)] + [(sign, d) for d in range(1, side_a) for sign in (1, -1)]
+
+    def along(k, sign, d, act):
+        @pl.when(inside(a + sign))
+        def _():
+            act(copy(k, row_of(a - sign * d, b, core), row_of(a + sign, b, core), z_sem.at[k, (sign + 1) // 2, d], d == 0))
+
+    def beside(k, sign, d, act):
+        origin = row_of(a - sign * d, b, core)
+        for e in range(1, side_b):
+            act(copy(k, origin, row_of(a, lax.rem(b + e, side_b), core), y_sem.at[k, a - sign * d, e], d == 0))
+
+    def to_core(k, origin, act, mine=False):
+        act(copy(k, origin, row_of(a, b, 1 - core), c_sem.at[k, origin // 2], mine))
+
+    def start(c):
+        c.start()
+
+    def finish(c):
+        c.wait_send()
+
     local = []
     for k in range(parts):
-        for d in range(1, side_a):
-            send(k, r, row_of(lax.rem(a + d, side_a), b, core), z_sem.at[k, d], mine=True)
-        for e in range(1, side_b):
-            send(k, r, row_of(a, lax.rem(b + e, side_b), core), y_sem.at[k, 0, e], mine=True)
-        send(k, r, row_of(a, b, 1 - core), c_sem.at[k, 0], mine=True)
+        along(k, 1, 0, start)
+        along(k, -1, 0, start)
+        beside(k, 1, 0, start)
+        to_core(k, r, start, True)
         c = pltpu.make_async_copy(own.at[pl.ds(k * group, group)], chunk(k, r), local_sem.at[k])
         c.start()
         local.append(c)
 
     def column(k):
-        for d in range(1, side_a):
-            origin = row_of(lax.rem(a + d, side_a), b, core)
-            arrived(k, origin)
-            for e in range(1, side_b):
-                send(k, origin, row_of(a, lax.rem(b + e, side_b), core), y_sem.at[k, d, e])
-            send(k, origin, row_of(a, b, 1 - core), c_sem.at[k, d])
+        for sign, d in hops[1:]:
+
+            @pl.when(inside(a - sign * d))
+            def _():
+                origin = row_of(a - sign * d, b, core)
+                arrived(k, origin)
+                along(k, sign, d, start)
+                beside(k, sign, d, start)
+                to_core(k, origin, start)
 
     def across(k):
-        for d in range(side_a):
-            for e in range(1, side_b):
-                origin = row_of(lax.rem(a + d, side_a), lax.rem(b + e, side_b), core)
-                arrived(k, origin)
-                send(k, origin, row_of(a, b, 1 - core), c_sem.at[k, e * side_a + d])
+        for sign, d in hops:
+
+            @pl.when(inside(a - sign * d))
+            def _():
+                for e in range(1, side_b):
+                    origin = row_of(a - sign * d, lax.rem(b + e, side_b), core)
+                    arrived(k, origin)
+                    to_core(k, origin, start)
 
     for k in range(parts):
         column(k)
@@ -110,13 +132,22 @@
             across(k - 1)
     across(parts - 1)
     for k in range(parts):
-        for d in range(side_a):
-            for e in range(side_b):
-                arrived(k, row_of(lax.rem(a + d, side_a), lax.rem(b + e, side_b), 1 - core))
+        along(k, 1, 0, finish)
+        along(k, -1, 0, finish)
+        beside(k, 1, 0, finish)
+        for sign, d in hops[1:]:
+
+            @pl.when(inside(a - sign * d))
+            def _():
+                along(k, sign, d, finish)
+                beside(k, sign, d, finish)
+
+        for a_ in range(side_a):
+            for b_ in range(side_b):
+                arrived(k, row_of(a_, b_, 1 - core))
+                to_core(k, row_of(a_, b_, core), finish)
     for c in local:
         c.wait()
-    for c in sent:
-        c.wait_send()
 
 
 def gather_history(history, rows, width):
@@ -129,16 +160,16 @@
         functools.partial(gather_kernel, side_a, side_b, group),
         out_shape=jax.ShapeDtypeStruct((lags, rows * per, exc, width), jnp.float32),
         in_specs=[pl.BlockSpec(memory_space=pltpu.VMEM)],
-        out_specs=pl.BlockSpec(memory_space=pl.ANY),
+        out_specs=pl.BlockSpec(memory_space=pltpu.VMEM),
         scratch_shapes=[
             pltpu.VMEM((lags, per, exc, width), jnp.float32),
             pltpu.SemaphoreType.DMA((parts,)),
-            pltpu.SemaphoreType.DMA((parts, side_a)),
+            pltpu.SemaphoreType.DMA((parts, 2, side_a)),
             pltpu.SemaphoreType.DMA((parts, side_a, side_b)),
             pltpu.SemaphoreType.DMA((parts, side_a * side_b)),
             pltpu.SemaphoreType.DMA((parts, rows)),
         ],
-        compiler_params=pltpu.CompilerParams(collective_id=0, has_side_effects=True),
+        compiler_params=pltpu.CompilerParams(collective_id=0, has_side_effects=True, vmem_limit_bytes=24 * MIB),
         name="gather_history",
     )(history)
 
@@ -195,7 +226,7 @@
     n = kernel.shape[0]
     width = kernel.shape[1]
     lags, blocks, exc, _ = panels.shape
-    slots = max(d for d in range(1, 13) if n % d == 0)
+    slots = max(d for d in range(1, 87) if n % d == 0)
     return pl.pallas_call(
         functools.partial(product_kernel, slots),
         out_shape=jax.ShapeDtypeStruct((blocks + 1, exc, width), jnp.float32),
@@ -203,13 +234,13 @@
             num_scalar_prefetch=2,
             grid=(n // slots,),
             in_specs=[
-                pl.BlockSpec(panels.shape, lambda s, *_: (0, 0, 0, 0), pipeline_mode=pl.Buffered(1)),
+                pl.BlockSpec(memory_space=pltpu.VMEM),
                 pl.BlockSpec((slots, width, width), lambda s, *_: (s, 0, 0)),
             ],
-            out_specs=pl.BlockSpec((blocks + 1, exc, width), lambda s, *_: (0, 0, 0)),
+            out_specs=pl.BlockSpec(memory_space=pltpu.VMEM),
         ),
         compiler_params=pltpu.CompilerParams(
-            dimension_semantics=("arbitrary",), vmem_limit_bytes=40 * MIB
+            dimension_semantics=("arbitrary",), vmem_limit_bytes=36 * MIB
         ),
         cost_estimate=pl.CostEstimate(
             flops=n * width * width * exc * 16,

time: 135 us -> 98.2 us (0.73)
  Pallas kernels: 129 us -> 95.1 us
  local copies, waits for them, and re-layouts: 5.06 us -> 2.72 us
    pallas_call x1, Pallas kernels: 38.4 us -> 19.7 us  [products(): pl.pallas_call(functools.partial(product_kernel, slots), out_shape=jax.Sh...]
    pallas_call x1, Pallas kernels: 28.1 us -> 20.3 us  [scatter_sum(): pl.pallas_call(functools.partial(scatter_kernel, side_a, side_b, per), ou...]
    pallas_call x1, Pallas kernels: 62.8 us -> 55.1 us  [gather_history(): pl.pallas_call(functools.partial(gather_kernel, side_a, side_b, group), o...]
    unnamed x6, local copies, waits for them, and re-layouts: 4.9 us -> 2.56 us
where the time goes in v2:
time: 98.2 us; the launch traced here: 97.9 us
  Pallas kernels  95.1 us (97%)
  local copies, waits for them, and re-layouts  2.72 us (3%)
    pallas_call x1, Pallas kernels, gather_history(): pl.pallas_call(functools.partial(gather_kernel, side_a, side_b, group), o...  55.1 us
    pallas_call x1, Pallas kernels, scatter_sum(): pl.pallas_call(functools.partial(scatter_kernel, side_a, side_b, per), ou...  20.3 us
    pallas_call x1, Pallas kernels, products(): pl.pallas_call(functools.partial(product_kernel, slots), out_shape=jax.Sh...  19.7 us
    unnamed x6, local copies, waits for them, and re-layouts  2.56 us

profile of v2, /device:TPU:0, one launch (start us, length us, event | category | flops | bytes accessed | tf_op | source)
XLA Modules:
  0.0 97.9 jit_solution(6068953333650221503)
XLA Ops:
  0.0 0.0 copy-start.1
  0.0 0.9 copy.5
  0.9 0.2 reshape.3.pairs
  1.0 0.0 copy-start
  1.1 1.0 %copy-done = f32[4,32,1024]{2,1,0:T(8,128)S(1)} copy-done((f32[4,32,1024]{2,1,0:T(8,128)S(1)}, f32[4,32,1024]{2,1,0:T(8,128)}, u32[]{:S(2)}) %copy-start) | copy-done | bytes 524312
  2.1 55.1 %gather_history.1.g_ref = f32[4,128,32,128]{3,2,1,0:T(8,128)S(1)} custom-call(f32[4,32,1024]{2,1,0:T(8,128)S(1)} %copy-done), custom_call_target="tpu_custom_call" | custom-call | tf_op jit(solution)/shard_map/gather_history/pallas_call | solution.py:159
  57.2 0.0 copy-done.1
  57.2 19.7 %block_products.1.t_ref = f32[129,32,128]{2,1,0:T(8,128)S(1)} custom-call(s32[1032]{0:T(1024)S(1)} %reshape.3.pairs, s32[128,128]{1,0:T(8,128)S(1)} %copy-done.1, f32[4,128,32,128]{3,2,1,0:T(8,128)S(1)} %gather_history.1.g_ref, f32[516,128,128]{2,1,0:T(8,128)} %k_ref.1), custom_call_target="tpu_custom_call" | custom-call | flops 4328521728 | bytes 42205184 | tf_op jit(solution)/shard_map/block_products/pallas_call | solution.py:230
  76.9 20.3 %scatter_sum.1 = f32[32,1024]{1,0:T(8,128)S(1)} custom-call(f32[129,32,128]{2,1,0:T(8,128)S(1)} %block_products.1.t_ref), custom_call_target="tpu_custom_call" | custom-call | tf_op jit(solution)/shard_map/scatter_sum/pallas_call | solution.py:336
  97.2 0.7 copy.7
Async XLA Ops:
  0.0 57.2 %copy-start.1 = (s32[128,128]{1,0:T(8,128)S(1)}, s32[128,128]{1,0:T(8,128)}, u32[]{:S(2)}) copy-start(s32[128,128]{1,0:T(8,128)} %lag.1) | copy-start | bytes 196612
  1.0 1.0 %copy-start = (f32[4,32,1024]{2,1,0:T(8,128)S(1)}, f32[4,32,1024]{2,1,0:T(8,128)}, u32[]{:S(2)}) copy-start(f32[4,32,1024]{2,1,0:T(8,128)} %h_ref.1) | copy-start | bytes 1572868

commit v3 on v2

--- a/solution.py
+++ b/solution.py
@@ -40,16 +40,21 @@
     pl.semaphore_wait(barrier, side_a + side_b - 1)
 
 
-def gather_kernel(side_a, side_b, group, h_ref, g_ref, own, local_sem, z_sem, y_sem, c_sem, recv_sem):
+def gather_kernel(side_a, side_b, group, h_ref, g_ref, own, own_sem, local_sem, z_sem, y_sem, c_sem, recv_sem):
     r, a, b, core = place(side_b)
     lags = h_ref.shape[0]
     width = g_ref.shape[3]
     per = h_ref.shape[2] // width
     parts = lags // group
+    loads = [
+        pltpu.make_async_copy(h_ref.at[:, :, pl.ds(m * width, width)], own.at[:, m], own_sem.at[m])
+        for m in range(per)
+    ]
+    for c in loads:
+        c.start()
     greet(side_a, side_b, a, b, core)
-    for k in range(lags):
-        for m in range(per):
-            own[k, m] = h_ref[k, :, m * width : (m + 1) * width]
+    for c in loads:
+        c.wait()
 
     def row_of(a_, b_, c_):
         return (a_ * side_b + b_) * 2 + c_
@@ -159,10 +164,11 @@
     return pl.pallas_call(
         functools.partial(gather_kernel, side_a, side_b, group),
         out_shape=jax.ShapeDtypeStruct((lags, rows * per, exc, width), jnp.float32),
-        in_specs=[pl.BlockSpec(memory_space=pltpu.VMEM)],
+        in_specs=[pl.BlockSpec(memory_space=pltpu.HBM)],
         out_specs=pl.BlockSpec(memory_space=pltpu.VMEM),
         scratch_shapes=[
             pltpu.VMEM((lags, per, exc, width), jnp.float32),
+            pltpu.SemaphoreType.DMA((per,)),
             pltpu.SemaphoreType.DMA((parts,)),
             pltpu.SemaphoreType.DMA((parts, 2, side_a)),
             pltpu.SemaphoreType.DMA((parts, side_a, side_b)),
@@ -197,8 +203,8 @@
 
     for q in range(slots):
         s = step * slots + q
-        i = pairs[2 * s]
-        j = pairs[2 * s + 1]
+        i = pairs[0, s]
+        j = pairs[1, s]
         live = i >= 0
         row = jnp.maximum(i, 0)
         col = jnp.maximum(j, 0)
@@ -248,7 +254,7 @@
             transcendentals=0,
         ),
         name="block_products",
-    )(slot_pairs.reshape(-1), lag_table, panels, kernel)
+    )(slot_pairs.T, lag_table, panels, kernel)
 
 
 def scatter_kernel(side_a, side_b, per, t_ref, o_ref, buf1, buf2, buf3, sum2, sum3, s1, r1, s2, r2, s3, r3):

time: 98.2 us -> 97.4 us (level)
  local copies, waits for them, and re-layouts: 2.72 us -> 1.71 us
    unnamed x6 -> x7, local copies, waits for them, and re-layouts: 2.56 us -> 1.71 us
where the time goes in v3:
time: 97.4 us; the launch traced here: 97.1 us
  Pallas kernels  95.3 us (98%)
  local copies, waits for them, and re-layouts  1.71 us (2%)
    pallas_call x1, Pallas kernels, gather_history(): pl.pallas_call(functools.partial(gather_kernel, side_a, side_b, group), o...  55.3 us
    pallas_call x1, Pallas kernels, scatter_sum(): pl.pallas_call(functools.partial(scatter_kernel, side_a, side_b, per), ou...  20.3 us
    pallas_call x1, Pallas kernels, products(): pl.pallas_call(functools.partial(product_kernel, slots), out_shape=jax.Sh...  19.8 us

profile of v3, /device:TPU:0, one launch (start us, length us, event | category | flops | bytes accessed | tf_op | source)
XLA Modules:
  0.0 97.1 jit_solution(9692707860986787816)
XLA Ops:
  0.0 0.0 copy-start
  0.0 1.0 %copy-done = f32[4,32,1024]{2,1,0:T(8,128)S(1)} copy-done((f32[4,32,1024]{2,1,0:T(8,128)S(1)}, f32[4,32,1024]{2,1,0:T(8,128)}, u32[]{:S(2)}) %copy-start) | copy-done | bytes 524312
  1.0 0.0 copy-start.1
  1.0 0.0 copy-start.2
  1.0 55.3 %gather_history.1.g_ref = f32[4,128,32,128]{3,2,1,0:T(8,128)S(1)} custom-call(f32[4,32,1024]{2,1,0:T(8,128)S(1)} %copy-done), custom_call_target="tpu_custom_call" | custom-call | tf_op jit(solution)/shard_map/gather_history/pallas_call | solution.py:164
  56.3 0.0 copy-done.1
  56.3 0.0 copy-done.2
  56.3 19.8 %block_products.1.t_ref = f32[129,32,128]{2,1,0:T(8,128)S(1)} custom-call(s32[2,516]{1,0:T(2,128)S(1)} %bitcast.1, s32[128,128]{1,0:T(8,128)S(1)} %copy-done.1, f32[4,128,32,128]{3,2,1,0:T(8,128)S(1)} %gather_history.1.g_ref, f32[516,128,128]{2,1,0:T(8,128)} %k_ref.1), custom_call_target="tpu_custom_call" | custom-call | flops 4328521728 | bytes 42205184 | tf_op jit(solution)/shard_map/block_products/pallas_call | solution.py:236
  76.1 20.3 %scatter_sum.1 = f32[32,1024]{1,0:T(8,128)S(1)} custom-call(f32[129,32,128]{2,1,0:T(8,128)S(1)} %block_products.1.t_ref), custom_call_target="tpu_custom_call" | custom-call | tf_op jit(solution)/shard_map/scatter_sum/pallas_call | solution.py:342
  96.4 0.7 copy.6
Async XLA Ops:
  0.0 1.0 %copy-start = (f32[4,32,1024]{2,1,0:T(8,128)S(1)}, f32[4,32,1024]{2,1,0:T(8,128)}, u32[]{:S(2)}) copy-start(f32[4,32,1024]{2,1,0:T(8,128)} %h_ref.1) | copy-start | bytes 1572868
  1.0 55.3 %copy-start.1 = (s32[128,128]{1,0:T(8,128)S(1)}, s32[128,128]{1,0:T(8,128)}, u32[]{:S(2)}) copy-start(s32[128,128]{1,0:T(8,128)} %lag.1) | copy-start | bytes 196612
  1.0 55.3 %copy-start.2 = (s32[516,2]{0,1:T(2,128)S(1)}, s32[516,2]{0,1:T(2,128)}, u32[]{:S(2)}) copy-start(s32[516,2]{0,1:T(2,128)} %param.4) | copy-start | bytes 12388
